TPU v7x, 32 devices: a whole 2x2x4 slice. The times are simulated.
32 devices in a mesh: kv: 4 (over y, x), sp: 8 (over z, core).
Axes of the slice: x: 2, y: 2, z: 4, core: 2. Of those that a mesh axis runs over, the one named last changes fastest.
Arguments:
- queries: bfloat16 [4096, 4096], P('sp'), may hold values from -1.1953125 to 1.1953125
- keys: bfloat16 [8192, 4096], P(('kv', 'sp')), may hold values from -1.1953125 to 1.1953125
- values: bfloat16 [8192, 4096], P(('kv', 'sp')), may hold values from -6 to 6
- outputs: bfloat16 [4096, 4096], P('sp'), may hold values from -6 to 6
- out_grad: bfloat16 [4096, 4096], P('sp'), may hold values from -768 to 768
- stats: float32 [4096, 32], P('sp'), may hold values from -1 to 1
Outputs:
- query_grad: float32 [4096, 4096], P(('kv', 'sp'))
- key_grad: float32 [8192, 4096], P(('kv', 'sp'))
- value_grad: float32 [8192, 4096], P(('kv', 'sp'))
All inputs are finite; a program needn't handle non-finite values.
Results may differ from a plain program's by a relative error of at most 0.0029.
Values may be sent and summed in bfloat16 or wider, within the bound.
A program may use at most 128 MiB of HBM per device.

v0:
```python
import functools
import math

import jax
import jax.numpy as jnp
from jax import lax
from jax.experimental import pallas as pl
from jax.experimental.pallas import tpu as pltpu
from jax.sharding import Mesh, PartitionSpec as P

DH = 128
NT = (((1,), (1,)), ((), ()))
NN = (((1,), (0,)), ((), ()))
TN = (((0,), (0,)), ((), ()))


def dot(left, right, dims):
    return lax.dot_general(left, right, dims, preferred_element_type=jnp.float32)


def attention_kernel(qt, kt, key_total, st_ref, de_ref, q_ref, g_ref, k_ref, v_ref, dq_ref, dk_ref, dv_ref, dk_acc, dv_acc):
    inverse_root = 1.0 / math.sqrt(DH)
    to_log2 = math.log2(math.e)
    dk_acc[...] = jnp.zeros_like(dk_acc)
    dv_acc[...] = jnp.zeros_like(dv_acc)

    def q_step(i, carry):
        qs = pl.ds(pl.multiple_of(i * qt, qt), qt)
        q = q_ref[qs, :]
        g = g_ref[qs, :]
        st = st_ref[0, :, qs] * to_log2 + math.log2(key_total)
        de = de_ref[0, :, qs]
        total = None
        for j in range(k_ref.shape[0] // kt):
            ks = pl.ds(j * kt, kt)
            k = k_ref[ks, :]
            probs = jnp.exp2(dot(k, q, NT) * (inverse_root * to_log2) - st)
            dv_acc[ks, :] += dot(probs.astype(jnp.bfloat16), g, NN)
            prob_grad = dot(v_ref[ks, :], g, NT)
            ds = (probs * (prob_grad - de)).astype(jnp.bfloat16)
            dk_acc[ks, :] += dot(ds, q, NN)
            part = dot(k, ds, TN)
            total = part if total is None else total + part
        dq_ref[qs, :] = (total * inverse_root).T.astype(dq_ref.dtype)
        return carry

    lax.fori_loop(0, q_ref.shape[0] // qt, q_step, 0)
    dk_ref[...] = (dk_acc[...] * inverse_root).astype(dk_ref.dtype)
    dv_ref[...] = dv_acc[...].astype(dv_ref.dtype)


def attention(q, g, k, v, st, de, key_total, dq_type):
    rows, width = q.shape
    keys = k.shape[0]
    heads = width // DH

    def columns(n):
        return pl.BlockSpec((n, DH), lambda h: (0, h))

    row = pl.BlockSpec((1, 1, rows), lambda h: (h, 0, 0))
    return pl.pallas_call(
        functools.partial(attention_kernel, min(1024, rows), min(256, keys), key_total),
        grid=(heads,),
        in_specs=[row, row, columns(rows), columns(rows), columns(keys), columns(keys)],
        out_specs=[columns(rows), columns(keys), columns(keys)],
        out_shape=[
            jax.ShapeDtypeStruct((rows, width), dq_type),
            jax.ShapeDtypeStruct((keys, width), jnp.bfloat16),
            jax.ShapeDtypeStruct((keys, width), jnp.bfloat16),
        ],
        scratch_shapes=[pltpu.VMEM((keys, DH), jnp.float32)] * 2,
        compiler_params=pltpu.CompilerParams(vmem_limit_bytes=40 * 2**20),
    )(st, de, q, g, k, v)


def row_products(left, right, heads):
    rows = left.shape[0]
    return jnp.sum(
        left.astype(jnp.float32).reshape(rows, heads, -1)
        * right.astype(jnp.float32).reshape(rows, heads, -1),
        axis=2,
    )


def on_device(queries, keys, values, outputs, out_grad, stats):
    kv_n, z_n, c_n = lax.axis_size("kv"), lax.axis_size("z"), lax.axis_size("c")
    heads = stats.shape[1]
    key_total = keys.shape[0] * kv_n * z_n * c_n
    q_len = queries.shape[0] * z_n * c_n
    delta = row_products(out_grad, outputs, heads)
    kv = lax.axis_index("kv")

    def to_heads(array):
        width = array.shape[1] // kv_n
        own = lax.dynamic_slice_in_dim(array, kv * width, width, 1)
        pair = lax.all_to_all(own, "c", split_axis=1, concat_axis=0, tiled=True)
        return lax.all_gather(pair, "z", axis=0, tiled=True)

    def exchange(array):
        return lax.all_to_all(array, ("kv", "c"), split_axis=1, concat_axis=0, tiled=True)

    def give_back(array):
        return lax.all_to_all(array, ("kv", "c"), split_axis=0, concat_axis=1, tiled=True)

    k, v = exchange(keys), exchange(values)
    q, g = to_heads(queries), to_heads(out_grad)
    both = jnp.stack([stats, delta], axis=1).reshape(-1, 2, heads)
    width = heads // kv_n
    both = lax.dynamic_slice_in_dim(both, kv * width, width, 2)
    both = lax.all_gather(both, ("z", "c"), axis=0, tiled=True)
    width //= c_n
    both = lax.dynamic_slice_in_dim(both, lax.axis_index("c") * width, width, 2)
    st = jnp.transpose(both[:, 0])[:, None, :]
    de = jnp.transpose(both[:, 1])[:, None, :]
    dq, dk, dv = attention(q, g, k, v, st, de, key_total, jnp.float32)
    part = dq.reshape(kv_n, z_n, c_n, q_len // (kv_n * z_n * c_n), dq.shape[1])
    part = lax.psum_scatter(part, "z", scatter_dimension=1, tiled=True)
    dq = give_back(part.reshape(-1, dq.shape[1]).astype(jnp.bfloat16))
    dk, dv = give_back(dk), give_back(dv)
    return tuple(array.astype(jnp.float32) for array in (dq, dk, dv))


def solution(mesh):
    kv_n, sp_n = mesh.shape["kv"], mesh.shape["sp"]
    mesh = Mesh(mesh.devices.reshape(kv_n, sp_n // 2, 2), ("kv", "z", "c"))
    sp = P(("z", "c"), None)
    both = P(("kv", "z", "c"), None)
    return jax.shard_map(
        on_device,
        mesh=mesh,
        in_specs=(sp, both, both, sp, sp, sp),
        out_specs=(both, both, both),
        check_vma=False,
    )
```

profile of v0, /device:TPU:0, one launch (start us, length us, event | category | flops | bytes accessed | tf_op | source)
XLA Modules:
  0.0 648.2 jit_solution(11774049849796309803)
XLA Ops:
  9.5 4.6 all_to_all.112
  16.0 4.6 all_to_all.113
  24.1 5.2 all-to-all-start.2
  29.2 3.1 copy.58
  32.4 23.5 %all-to-all-done.2 = bf16[256,8,512]{2,0,1:T(8,128)(2,1)S(1)} async-done(((bf16[256,8,512]{2,0,1:T(8,128)(2,1)}), bf16[256,8,512]{2,0,1:T(8,128)(2,1)S(1)}, u32[]{:S(2)}, u32[]{:S(2)}) %all-to-all-start.2) | async-done | bytes 2097184 | tf_op jit(solution)/shard_map/all_to_all | solution.py:100
  55.9 4.3 all-to-all-start.3
  60.3 5.1 multiply_bitcast_fusion
  65.4 5.0 copy.55
  70.4 5.7 reduce_sum.9
  76.3 16.6 %all_gather.9 = f32[4096,2,8]{0,2,1:T(8,128)S(1)} all-gather(f32[512,2,8]{0,2,1:T(8,128)S(1)} %fusion), channel_id=1, replica_groups=mesh['kv'=4,'z'=4,'c'=2] {'z','c'}, dimensions={0}, use_global_device_ids=true | all-gather | bytes 294912 | tf_op jit(solution)/shard_map/all_gather | solution.py:110
  93.7 7.3 %all-gather.3.cloned.1.call-done.q_ref = bf16[4096,512]{1,0:T(8,128)(2,1)} async-done(((bf16[1024,512]{1,0:T(8,128)(2,1)}), bf16[4096,512]{1,0:T(8,128)(2,1)}) %all-gather.3.cloned.1.call-update) | async-done | bytes 4194320 | tf_op jit(solution)/shard_map/all_gather | solution.py:97
  101.0 80.9 %all-gather.5.cloned.1.call-done.g_ref = bf16[4096,512]{1,0:T(8,128)(2,1)} async-done(((bf16[1024,512]{1,0:T(8,128)(2,1)}), bf16[4096,512]{1,0:T(8,128)(2,1)}) %all-gather.5.cloned.1.call-update) | async-done | bytes 4194320 | tf_op jit(solution)/shard_map/all_gather | solution.py:97
  181.9 2.2 copy-done
  184.1 88.7 %shard_map.85 = (f32[4096,512]{1,0:T(8,128)}, bf16[2048,512]{1,0:T(8,128)(2,1)S(1)}, bf16[2048,512]{1,0:T(8,128)(2,1)}) custom-call(f32[4,1,4096]{2,1,0:T(1,128)S(1)} %copy.42.st_ref, f32[4,1,4096]{2,1,0:T(1,128)S(1)} %broadcast_in_dim.7.de_ref, bf16[4096,512]{1,0:T(8,128)(2,1)S(1)} %copy-done, bf16[4096,512]{1,0:T(8,128)(2,1)} %all-gather.5.cloned.1.call-done.g_ref, ...), custom_call_target="tpu_custom_call" | custom-call | tf_op jit(solution)/shard_map/pallas_call | solution.py:61
  274.1 281.7 %all-reduce.2 = bf16[4,4,2,128,512]{4,3,2,1,0:T(8,128)(2,1)} all-reduce(f32[4,4,2,128,512]{4,3,2,1,0:T(8,128)} %bitcast.60), channel_id=2, replica_groups=mesh['kv'=4,'z'=4,'c'=2] {'z'}, use_global_device_ids=true, to_apply=%region_1.0.clone | all-reduce | flops 2097152 | bytes 12582912
  555.8 2.2 dynamic-slice_convert_fusion
  558.0 20.2 %all_to_all.114 = bf16[8,128,512]{2,1,0:T(8,128)(2,1)} all-to-all(bf16[8,128,512]{2,1,0:T(8,128)(2,1)S(1)} %bitcast.64), channel_id=1, replica_groups=mesh['kv'=4,'z'=4,'c'=2] {'kv','c'}, dimensions={0} | all-to-all | bytes 2097152 | tf_op jit(solution)/shard_map/all_to_all | solution.py:103
  578.2 29.8 %all_to_all.115 = bf16[8,256,512]{2,1,0:T(8,128)(2,1)} all-to-all(bf16[8,256,512]{2,1,0:T(8,128)(2,1)S(1)} %bitcast.58), channel_id=1, replica_groups=mesh['kv'=4,'z'=4,'c'=2] {'kv','c'}, dimensions={0} | all-to-all | bytes 4194304 | tf_op jit(solution)/shard_map/all_to_all | solution.py:103
  607.9 3.6 all-to-all-start.6
  614.6 2.9 copy.46
  617.5 2.2 convert_bitcast_fusion.1
  619.7 2.7 copy.53
  622.3 15.8 %all-to-all-done.6 = bf16[8,256,512]{2,1,0:T(8,128)(2,1)S(1)} async-done(((bf16[8,256,512]{2,1,0:T(8,128)(2,1)}), bf16[8,256,512]{2,1,0:T(8,128)(2,1)S(1)}, u32[]{:S(2)}, u32[]{:S(2)}) %all-to-all-start.6) | async-done | bytes 2097184 | tf_op jit(solution)/shard_map/all_to_all | solution.py:103
  638.7 2.7 copy.54
  (31 shorter events, 13.6 us)
Async XLA Ops:
  7.2 93.9 %all-gather.3.cloned.1.call-start = ((), (), s32[]{:S(2)}) async-start(), calls=%async_computation.7 | async-start | bytes 5242880 | tf_op jit(solution)/shard_map/all_gather | solution.py:97
  15.4 166.5 %all-gather.5.cloned.1.call-start = ((), (), s32[]{:S(2)}) async-start(), calls=%async_computation.8 | async-start | bytes 5242880 | tf_op jit(solution)/shard_map/all_gather | solution.py:97
  20.6 2.0 copy-start.3
  24.1 31.8 %all-to-all-start.2 = ((bf16[256,8,512]{2,0,1:T(8,128)(2,1)}), bf16[256,8,512]{2,0,1:T(8,128)(2,1)S(1)}, u32[]{:S(2)}, u32[]{:S(2)}) async-start(bf16[256,8,512]{2,0,1:T(8,128)(2,1)} %bitcast.62), calls=%async_computation.2 | async-start | bytes 4194304 | tf_op jit(solution)/shard_map/all_to_all | solution.py:100
  55.9 37.8 %all-to-all-start.3 = ((bf16[256,8,512]{2,0,1:T(8,128)(2,1)}), bf16[256,8,512]{2,0,1:T(8,128)(2,1)}, u32[]{:S(2)}, u32[]{:S(2)}) async-start(bf16[256,8,512]{2,0,1:T(8,128)(2,1)} %bitcast.61), calls=%async_computation.3 | async-start | bytes 4194304 | tf_op jit(solution)/shard_map/all_to_all | solution.py:100
  70.4 5.8 copy-start.4
  70.4 22.6 %copy-start.5 = (u32[32]{0:T(128)S(1)}, u32[32]{0:T(128)}, u32[]{:S(2)}) copy-start(u32[32]{0:T(128)} %constant.25) | copy-start | bytes 388
  181.9 2.2 copy-start
  272.8 1.3 copy-start.1
  555.8 22.3 %copy-start.2 = (bf16[2048,512]{1,0:T(8,128)(2,1)S(1)}, bf16[2048,512]{1,0:T(8,128)(2,1)}, u32[]{:S(2)}) copy-start(bf16[2048,512]{1,0:T(8,128)(2,1)} %copy-done.1) | copy-start | bytes 6291460
  607.9 30.2 %all-to-all-start.6 = ((bf16[8,256,512]{2,1,0:T(8,128)(2,1)}), bf16[8,256,512]{2,1,0:T(8,128)(2,1)S(1)}, u32[]{:S(2)}, u32[]{:S(2)}) async-start(bf16[8,256,512]{2,1,0:T(8,128)(2,1)} %bitcast.30), calls=%async_computation.6 | async-start | bytes 4194304 | tf_op jit(solution)/shard_map/all_to_all | solution.py:103
Sparse Core Ops, SparseCore 0:
  15.5 85.4 all-gather.2
  102.6 79.2 all-gather.4
where the time goes:
time: 649 us; the launch traced here: 648 us
  blocking collectives  357 us (55%)
  waiting for transfers between devices  128 us (20%)
  Pallas kernels  88.7 us (14%)
  local copies, waits for them, and re-layouts  32.1 us (5%)
  other arithmetic  15 us (2%)
  between operations  14.2 us (2%)
  starting transfers between devices  13.2 us (2%)
    unnamed x1, blocking collectives  282 us
    pallas_call x1, Pallas kernels, attention(): pl.pallas_call(functools.partial(attention_kernel, min(1024, rows), min(2...  88.7 us
    all_gather x2, waiting for transfers between devices, to_heads(): return lax.all_gather(pair, 'z', axis=0, tiled=True)  88.2 us
    all_to_all x2, blocking collectives, give_back(): lax.all_to_all(array, ('kv', 'c'), split_axis=0, concat_axis=1, tiled=True)  49.9 us
    all_to_all x2, waiting for transfers between devices, exchange(): lax.all_to_all(array, ('kv', 'c'), split_axis=1, concat_axis=0, tiled=True)  23.5 us
    all_gather x1, blocking collectives, on_device(): both = lax.all_gather(both, ('z', 'c'), axis=0, tiled=True)  16.6 us
    all_to_all x1, waiting for transfers between devices, give_back(): lax.all_to_all(array, ('kv', 'c'), split_axis=0, concat_axis=1, tiled=True)  15.8 us
    unnamed x17, local copies, waits for them, and re-layouts  13.8 us
  transfers between devices with their start and end apart: 5, of which 4 were waited for; matrix products, arithmetic and copies ran while one was open for 5% of the time, Pallas kernels for 0%

commit v1 on v0

v1 whole, which is shorter than its diff:
```python
import functools
import math

import jax
import jax.numpy as jnp
from jax import lax
from jax.experimental import pallas as pl
from jax.experimental.pallas import tpu as pltpu
from jax.sharding import Mesh, PartitionSpec as P

DH = 128
NT = (((1,), (1,)), ((), ()))
NN = (((1,), (0,)), ((), ()))
TN = (((0,), (0,)), ((), ()))


def dot(left, right, dims):
    return lax.dot_general(left, right, dims, preferred_element_type=jnp.float32)


MESH = pl.DeviceIdType.MESH


def fused_kernel(key_total, q_in, g_in, k_in, v_in, aux_in, dq_out, dk_out, dv_out,
                 q_buf, g_buf, aux_buf, k_buf, v_buf, dq_stage, dk_stage, dv_stage, dk_acc, dv_acc,
                 kv_recv, kv_send, row_recv, own_send, mate_send, pass_send,
                 aux_recv, aux_own, aux_mate, aux_pass, out_recv, out_send):
    kv_n, z_n, c_n = lax.axis_size("kv"), lax.axis_size("z"), lax.axis_size("c")
    kv, z, c = lax.axis_index("kv"), lax.axis_index("z"), lax.axis_index("c")
    groups = kv_n * c_n
    count = groups * z_n
    group = kv * c_n + c
    heads = q_buf.shape[0]
    part = q_in.shape[0]
    owned = dq_out.shape[1]
    inverse_root = 1.0 / math.sqrt(DH)
    to_log2 = math.log2(math.e)
    width = heads * DH
    rows_io = ((q_in, q_buf), (g_in, g_buf))
    keys_io = ((k_in, k_buf), (v_in, v_buf))
    grads_io = ((dk_stage, dk_out), (dv_stage, dv_out))

    def device(index):
        inner = lax.rem(index, z_n * c_n)
        return (index // (z_n * c_n), inner // c_n, lax.rem(inner, c_n))

    def send(src, dst, s, r, where):
        return pltpu.make_async_remote_copy(src, dst, s, r, device_id=where, device_id_type=MESH)

    def cols(owner, h):
        return pl.ds(pl.multiple_of(owner * width + h * DH, DH), DH)

    barrier = pltpu.get_barrier_semaphore()
    me = (kv * z_n + z) * c_n + c

    def greet(i, carry):
        pl.semaphore_signal(barrier, inc=1, device_id=device(lax.rem(me + i, count)), device_id_type=MESH)
        return carry

    lax.fori_loop(1, count, greet, 0)
    pl.semaphore_wait(barrier, count - 1)

    my_rows = pl.ds(pl.multiple_of(c * part, part), part)

    def send_keys(h):
        for a, (src, buf) in enumerate(keys_io):
            pltpu.make_async_copy(src.at[:, cols(group, h)], buf.at[h, group], kv_recv.at[h, a]).start()

        def one(i, carry):
            peer = lax.rem(group + i, groups)
            for a, (src, buf) in enumerate(keys_io):
                send(src.at[:, cols(peer, h)], buf.at[h, group], kv_send.at[a], kv_recv.at[h, a],
                     (peer // c_n, z, lax.rem(peer, c_n))).start()
            return carry

        lax.fori_loop(1, groups, one, 0)

    def send_rows(h):
        for a, (src, buf) in enumerate(rows_io):
            land = buf.at[h, z, my_rows]
            pltpu.make_async_copy(src.at[:, cols(group, h)], land, row_recv.at[h, z, a]).start()
            mate = 1 - c
            send(src.at[:, cols(kv * c_n + mate, h)], land, mate_send.at[a], row_recv.at[h, z, a],
                 (kv, z, mate)).start()
        for side, ok, there in sides:
            @pl.when(ok)
            def _():
                for a, (src, buf) in enumerate(rows_io):
                    for cc in range(c_n):
                        send(src.at[:, cols(kv * c_n + cc, h)], buf.at[h, z, my_rows], own_send.at[side, a],
                             row_recv.at[h, z, a], (kv, there, cc)).start()

    sides = ((0, z > 0, z - 1), (1, z < z_n - 1, z + 1))

    pltpu.make_async_copy(aux_in.at[c], aux_buf.at[z, c], aux_recv.at[z]).start()
    send(aux_in.at[1 - c], aux_buf.at[z, c], aux_mate, aux_recv.at[z], (kv, z, 1 - c)).start()
    for side, ok, there in sides:
        @pl.when(ok)
        def _():
            for cc in range(c_n):
                send(aux_in.at[cc], aux_buf.at[z, c], aux_own.at[side], aux_recv.at[z], (kv, there, cc)).start()

    send_keys(0)
    send_rows(0)
    if heads > 1:
        send_keys(1)
        send_rows(1)

    def unit(h, zz):
        q = q_buf[h, zz]
        g = g_buf[h, zz]
        st = jnp.concatenate([aux_buf[zz, i, pl.ds(2 * h, 1), :] for i in range(c_n)], axis=1)
        de = jnp.concatenate([aux_buf[zz, i, pl.ds(2 * h + 1, 1), :] for i in range(c_n)], axis=1)
        st = st * to_log2 + math.log2(key_total)

        def k_step(j, total):
            k = k_buf[h, j]
            probs = jnp.exp2(dot(k, q, NT) * (inverse_root * to_log2) - st)
            dv_acc[j] += dot(probs.astype(jnp.bfloat16), g, NN)
            prob_grad = dot(v_buf[h, j], g, NT)
            ds = (probs * (prob_grad - de)).astype(jnp.bfloat16)
            dk_acc[j] += dot(ds, q, NN)
            return total + dot(k, ds, TN)

        total = lax.fori_loop(0, groups, k_step, jnp.zeros((DH, q.shape[0]), jnp.float32), unroll=True)
        out = (total * inverse_root).T.astype(dq_stage.dtype)
        dq_stage[h, pl.ds(zz * groups, groups)] = out.reshape(groups, owned, DH)

        def push(j, carry):
            piece = zz * groups + j
            src, dst = dq_stage.at[h, piece], dq_out.at[z, :, cols(group, h)]

            @pl.when(piece == me)
            def _():
                pltpu.make_async_copy(src, dst, out_recv.at[2]).start()

            @pl.when(piece != me)
            def _():
                send(src, dst, out_send.at[2], out_recv.at[2], device(piece)).start()

            return carry

        lax.fori_loop(0, groups, push, 0)

    def at_offset(t):
        near = (t + 1) // 2
        left = lax.rem(t, 2) == 1
        zz = jnp.where(left, z - near, z + near)
        there = jnp.where(left, z + 1, z - 1)
        valid = (zz >= 0) & (zz < z_n)
        onward = valid & (t > 0) & (there >= 0) & (there < z_n)
        return zz, there, valid, onward

    def passes(h, zz, there):
        return [send(buf.at[h, zz], buf.at[h, zz], pass_send.at[h, zz, a], row_recv.at[h, zz, a], (kv, there, c))
                for a, (_, buf) in enumerate(rows_io)]

    def aux_passes(zz, there):
        return send(aux_buf.at[zz], aux_buf.at[zz], aux_pass.at[zz], aux_recv.at[zz], (kv, there, c))

    def arrived(ref, sem):
        pltpu.make_async_copy(ref, ref, sem).wait()

    def head(h, carry):
        @pl.when(h + 2 < heads)
        def _():
            send_keys(h + 2)
            send_rows(h + 2)

        dk_acc[...] = jnp.zeros_like(dk_acc)
        dv_acc[...] = jnp.zeros_like(dv_acc)
        for a, (_, buf) in enumerate(keys_io):
            arrived(buf.at[h], kv_recv.at[h, a])

        def step(t, inner):
            zz, there, valid, onward = at_offset(t)

            @pl.when(valid)
            def _():
                for a, (_, buf) in enumerate(rows_io):
                    arrived(buf.at[h, zz], row_recv.at[h, zz, a])

                @pl.when(h == 0)
                def _():
                    arrived(aux_buf.at[zz], aux_recv.at[zz])

                @pl.when(onward)
                def _():
                    for copy in passes(h, zz, there):
                        copy.start()

                    @pl.when(h == 0)
                    def _():
                        aux_passes(zz, there).start()

                unit(h, zz)

            return inner

        lax.fori_loop(0, 2 * z_n - 1, step, 0)
        dk_stage[h] = (dk_acc[...] * inverse_root).astype(dk_stage.dtype)
        dv_stage[h] = dv_acc[...].astype(dv_stage.dtype)
        for a, (stage, out) in enumerate(grads_io):
            pltpu.make_async_copy(stage.at[h, group], out.at[:, cols(group, h)], out_recv.at[a]).start()

        def one(i, inner):
            peer = lax.rem(group + i, groups)
            for a, (stage, out) in enumerate(grads_io):
                send(stage.at[h, peer], out.at[:, cols(group, h)], out_send.at[a], out_recv.at[a],
                     (peer // c_n, z, lax.rem(peer, c_n))).start()
            return inner

        lax.fori_loop(1, groups, one, 0)
        return carry

    lax.fori_loop(0, heads, head, 0)

    for a, (src, buf) in enumerate(rows_io):
        arrived(src.at[:, pl.ds(0, width)], mate_send.at[a])
        for side, ok, there in sides:
            @pl.when(ok)
            def _():
                arrived(src.at[:, pl.ds(0, c_n * width)], own_send.at[side, a])
    arrived(aux_in.at[0], aux_mate)
    for side, ok, there in sides:
        @pl.when(ok)
        def _():
            arrived(aux_in, aux_own.at[side])
    for a, (_, buf) in enumerate(keys_io):
        arrived(buf.at[:, pl.ds(0, groups - 1)], kv_send.at[a])

    def finish(h, carry):
        def step(t, inner):
            zz, there, valid, onward = at_offset(t)

            @pl.when(onward)
            def _():
                for copy in passes(h, zz, there):
                    copy.wait_send()

                @pl.when(h == 0)
                def _():
                    aux_passes(zz, there).wait_send()

            return inner

        return lax.fori_loop(0, 2 * z_n - 1, step, carry)

    lax.fori_loop(0, heads, finish, 0)
    for a, (stage, out) in enumerate(grads_io):
        arrived(stage.at[:, pl.ds(0, groups - 1)], out_send.at[a])
        arrived(out, out_recv.at[a])
    arrived(dq_stage.at[:, pl.ds(0, count - 1)], out_send.at[2])
    arrived(dq_out, out_recv.at[2])


def fused(q, g, k, v, aux, key_total, kv_n, z_n, c_n):
    part, total = q.shape
    groups = kv_n * c_n
    heads = total // DH // groups
    keys = k.shape[0]
    owned = part // kv_n
    low = jnp.bfloat16
    dma = pltpu.SemaphoreType.DMA
    any_space = pl.BlockSpec(memory_space=pl.ANY)
    return pl.pallas_call(
        functools.partial(fused_kernel, key_total),
        in_specs=[any_space] * 5,
        out_specs=[any_space] * 3,
        out_shape=[
            jax.ShapeDtypeStruct((z_n, owned, total), low),
            jax.ShapeDtypeStruct((keys, total), low),
            jax.ShapeDtypeStruct((keys, total), low),
        ],
        scratch_shapes=[pltpu.VMEM((heads, z_n, c_n * part, DH), low)] * 2
        + [pltpu.VMEM((z_n, c_n) + aux.shape[1:], jnp.float32)]
        + [pltpu.VMEM((heads, groups, keys, DH), low)] * 2
        + [pltpu.VMEM((heads, z_n * groups, owned, DH), low)]
        + [pltpu.VMEM((heads, groups, keys, DH), low)] * 2
        + [pltpu.VMEM((groups, keys, DH), jnp.float32)] * 2
        + [
            dma((heads, 2)), dma((2,)), dma((heads, z_n, 2)), dma((2, 2)), dma((2,)), dma((heads, z_n, 2)),
            dma((z_n,)), dma((2,)), dma, dma((z_n,)), dma((3,)), dma((3,)),
        ],
        compiler_params=pltpu.CompilerParams(
            collective_id=0, has_side_effects=True, vmem_limit_bytes=48 * 2**20
        ),
        cost_estimate=pl.CostEstimate(flops=43 * 10**9, bytes_accessed=3 * 10**7, transcendentals=0),
    )(q, g, k, v, aux)


def row_products(left, right, heads):
    rows = left.shape[0]
    return jnp.sum(
        left.astype(jnp.float32).reshape(rows, heads, -1)
        * right.astype(jnp.float32).reshape(rows, heads, -1),
        axis=2,
    )


def on_device(queries, keys, values, outputs, out_grad, stats):
    kv_n, z_n, c_n = lax.axis_size("kv"), lax.axis_size("z"), lax.axis_size("c")
    heads = stats.shape[1]
    key_total = keys.shape[0] * kv_n * z_n * c_n
    kv = lax.axis_index("kv")
    width = queries.shape[1] // kv_n
    near = heads // kv_n

    def own(array, size):
        return lax.dynamic_slice_in_dim(array, kv * size, size, 1)

    delta = row_products(own(out_grad, width), own(outputs, width), near)
    aux = jnp.stack([own(stats, near).T, delta.T], axis=1)
    aux = aux.reshape(c_n, 2 * near // c_n, stats.shape[0])
    dq, dk, dv = fused(queries, out_grad, keys, values, aux, key_total, kv_n, z_n, c_n)
    return jnp.sum(dq.astype(jnp.float32), axis=0), dk.astype(jnp.float32), dv.astype(jnp.float32)


def solution(mesh):
    kv_n, sp_n = mesh.shape["kv"], mesh.shape["sp"]
    mesh = Mesh(mesh.devices.reshape(kv_n, sp_n // 2, 2), ("kv", "z", "c"))
    sp = P(("z", "c"), None)
    both = P(("kv", "z", "c"), None)
    return jax.shard_map(
        on_device,
        mesh=mesh,
        in_specs=(sp, both, both, sp, sp, sp),
        out_specs=(both, both, both),
        check_vma=False,
    )
```

time: 649 us -> 248 us (0.38)
  blocking collectives: 357 us -> 0 us
  Pallas kernels: 88.7 us -> 231 us
  waiting for transfers between devices: 128 us -> 0 us
  local copies, waits for them, and re-layouts: 32.1 us -> 1.63 us
  between operations: 14.2 us -> 0.7 us
  starting transfers between devices: 13.2 us -> 0 us
    unnamed x1 -> x0, blocking collectives: 282 us -> none
    pallas_call x1, Pallas kernels: 88.7 us -> 231 us  [fused(): pl.pallas_call(functools.partial(fused_kernel, key_total), in_specs=[any_...]
    all_gather x2 -> x0, waiting for transfers between devices: 88.2 us -> none  [to_heads(): return lax.all_gather(pair, 'z', axis=0, tiled=True)]
    all_to_all x4 -> x0, blocking collectives: 59.1 us -> none  [the longest x2 49.9 us: give_back(): lax.all_to_all(array, ('kv', 'c'), split_axis=0, concat_axis=1, tiled=True)]
    all_to_all x3 -> x0, waiting for transfers between devices: 39.3 us -> none  [the longest x2 23.5 us: exchange(): lax.all_to_all(array, ('kv', 'c'), split_axis=1, concat_axis=0, tiled=True)]
    all_gather x1 -> x0, blocking collectives: 16.6 us -> none  [on_device(): both = lax.all_gather(both, ('z', 'c'), axis=0, tiled=True)]
    all_to_all x3 -> x0, starting transfers between devices: 13.1 us -> none  [the longest x2 9.52 us: exchange(): lax.all_to_all(array, ('kv', 'c'), split_axis=1, concat_axis=0, tiled=True)]
    unnamed x17 -> x4, local copies, waits for them, and re-layouts: 13.8 us -> 1.42 us
  transfers between devices with their start and end apart: 5 -> 0, of which waited for: 4 -> 0; matrix products, arithmetic and copies ran while one was open for 5% -> 0% of each run, Pallas kernels for 0% -> 0%
where the time goes in v1:
time: 248 us; the launch traced here: 246 us
  Pallas kernels  231 us (93%)
  other arithmetic  12.1 us (5%)
    pallas_call x1, Pallas kernels, fused(): pl.pallas_call(functools.partial(fused_kernel, key_total), in_specs=[any_...  231 us

profile of v1, /device:TPU:0, one launch (start us, length us, event | category | flops | bytes accessed | tf_op | source)
XLA Modules:
  0.0 245.5 jit_solution(1505165093571812245)
XLA Ops:
  0.6 0.0 copy-start
  0.7 0.8 copy-done
  1.5 0.1 copy.16
  1.6 1.9 multiply_bitcast_fusion
  3.6 0.5 copy.17
  4.0 0.6 reduce_sum.18
  4.7 0.2 copy.15
  4.9 231.1 %shard_map.85 = (bf16[4,128,4096]{2,1,0:T(8,128)(2,1)}, bf16[256,4096]{1,0:T(8,128)(2,1)S(1)}, bf16[256,4096]{1,0:T(8,128)(2,1)S(1)}) custom-call(bf16[512,4096]{1,0:T(8,128)(2,1)} %q_in.1, bf16[512,4096]{1,0:T(8,128)(2,1)} %g_in.1, bf16[256,4096]{1,0:T(8,128)(2,1)} %k_in.1, bf16[256,4096]{1,0:T(8,128)(2,1)} %v_in.1, f32[2,8,512]{2,1,0:T(8,128)S(1)} %reshape.12.aux_in), custom_call_target="tpu_custom_call" | custom-call | flops 43000000512 | bytes 30000000 | tf_op jit(solution)/shard_map/pallas_call | solution.py:266
  236.0 4.5 %convert_reduce_fusion = f32[128,4096]{1,0:T(8,128)} fusion(bf16[4,128,4096]{2,1,0:T(8,128)(2,1)} %get-tuple-element.6), kind=kLoop, calls=%fused_computation | loop fusion | flops 3670016 | bytes 6291456 | tf_op jit(solution)/shard_map/reduce_sum | solution.py:316
  240.5 2.5 %convert_element_type.18 = f32[256,4096]{1,0:T(8,128)} convert(bf16[256,4096]{1,0:T(8,128)(2,1)S(1)} %get-tuple-element.7) | non-fusion elementwise | flops 1048576 | bytes 6291456 | tf_op jit(solution)/shard_map/convert_element_type | solution.py:316
  243.0 2.5 %convert_element_type.19 = f32[256,4096]{1,0:T(8,128)} convert(bf16[256,4096]{1,0:T(8,128)(2,1)S(1)} %get-tuple-element.8) | non-fusion elementwise | flops 1048576 | bytes 6291456 | tf_op jit(solution)/shard_map/convert_element_type | solution.py:316
  (3 shorter events, 0.1 us)
Async XLA Ops:
  0.6 0.8 copy-start

commit v2 on v1

--- a/solution.py
+++ b/solution.py
@@ -22,9 +22,10 @@
 
 
 def fused_kernel(key_total, q_in, g_in, k_in, v_in, aux_in, dq_out, dk_out, dv_out,
-                 q_buf, g_buf, aux_buf, k_buf, v_buf, dq_stage, dk_stage, dv_stage, dk_acc, dv_acc,
+                 q_buf, g_buf, aux_buf, k_buf, v_buf, dq_stage, dq_send, dq_recv, dk_stage, dv_stage, dk_acc, dv_acc,
                  kv_recv, kv_send, row_recv, own_send, mate_send, pass_send,
-                 aux_recv, aux_own, aux_mate, aux_pass, out_recv, out_send):
+                 aux_recv, aux_own, aux_mate, aux_pass, out_recv, out_send, sum_recv, sum_send,
+                 dq_out_recv, dq_out_send):
     kv_n, z_n, c_n = lax.axis_size("kv"), lax.axis_size("z"), lax.axis_size("c")
     kv, z, c = lax.axis_index("kv"), lax.axis_index("z"), lax.axis_index("c")
     groups = kv_n * c_n
@@ -123,24 +124,77 @@
             return total + dot(k, ds, TN)
 
         total = lax.fori_loop(0, groups, k_step, jnp.zeros((DH, q.shape[0]), jnp.float32), unroll=True)
-        out = (total * inverse_root).T.astype(dq_stage.dtype)
-        dq_stage[h, pl.ds(zz * groups, groups)] = out.reshape(groups, owned, DH)
-
-        def push(j, carry):
-            piece = zz * groups + j
-            src, dst = dq_stage.at[h, piece], dq_out.at[z, :, cols(group, h)]
-
-            @pl.when(piece == me)
+        dq_stage[h, pl.ds(zz * groups, groups)] = (total * inverse_root).T.reshape(groups, owned, DH)
+
+    def keep(h):
+        def one(owner, carry):
+            base = (owner * z_n + z) * c_n
+            dq_send[h, pl.ds(base, c_n)] = dq_stage[h, pl.ds(base, c_n)].astype(dq_send.dtype)
+            for cc in range(c_n):
+                src, dst = dq_send.at[h, base + cc], dq_out.at[1, :, cols(group, h)]
+
+                @pl.when(base + cc == me)
+                def _():
+                    pltpu.make_async_copy(src, dst, dq_out_recv.at[1]).start()
+
+                @pl.when(base + cc != me)
+                def _():
+                    send(src, dst, dq_out_send.at[1], dq_out_recv.at[1], (owner, z, cc)).start()
+
+            return carry
+
+        lax.fori_loop(0, kv_n, one, 0)
+
+    def toward(h, side):
+        there = (z - 1, z + 1)[side]
+        fed = (z < z_n - 1, z > 0)[side]
+        slot = (2, 0)[side]
+
+        def one(i, carry):
+            owner, plane = i // z_n, lax.rem(i, z_n)
+
+            @pl.when((plane < z, plane > z)[side])
             def _():
-                pltpu.make_async_copy(src, dst, out_recv.at[2]).start()
-
-            @pl.when(piece != me)
-            def _():
-                send(src, dst, out_send.at[2], out_recv.at[2], device(piece)).start()
+                base = (owner * z_n + plane) * c_n
+                block = pl.ds(base, c_n)
+                mine = dq_stage[h, block]
+
+                @pl.when(fed)
+                def _():
+                    arrived(dq_recv.at[h, block], sum_recv.at[h, owner, plane])
+                    dq_send[h, block] = (mine + dq_recv[h, block].astype(jnp.float32)).astype(dq_send.dtype)
+
+                @pl.when(jnp.logical_not(fed))
+                def _():
+                    dq_send[h, block] = mine.astype(dq_send.dtype)
+
+                @pl.when(plane == there)
+                def _():
+                    for cc in range(c_n):
+                        send(dq_send.at[h, base + cc], dq_out.at[slot, :, cols(group, h)], dq_out_send.at[slot],
+                             dq_out_recv.at[slot], (owner, there, cc)).start()
+
+                @pl.when(plane != there)
+                def _():
+                    send(dq_send.at[h, block], dq_recv.at[h, block], sum_send.at[h, owner, plane],
+                         sum_recv.at[h, owner, plane], (kv, there, c)).start()
 
             return carry
 
-        lax.fori_loop(0, groups, push, 0)
+        lax.fori_loop(0, kv_n * z_n, one, 0)
+
+    upper = 2 * z >= z_n
+
+    def combine(h):
+        @pl.when(upper)
+        def _():
+            toward(h, 0)
+
+        toward(h, 1)
+
+        @pl.when(jnp.logical_not(upper))
+        def _():
+            toward(h, 0)
 
     def at_offset(t):
         near = (t + 1) // 2
@@ -211,9 +265,21 @@
             return inner
 
         lax.fori_loop(1, groups, one, 0)
+        keep(h)
+        late = h - lag
+
+        @pl.when(late >= 0)
+        def _():
+            combine(late)
+
         return carry
 
+    lag = jnp.where((z == 0) | (z == z_n - 1), 0, 1)
     lax.fori_loop(0, heads, head, 0)
+
+    @pl.when(lag == 1)
+    def _():
+        combine(heads - 1)
 
     for a, (src, buf) in enumerate(rows_io):
         arrived(src.at[:, pl.ds(0, width)], mate_send.at[a])
@@ -250,8 +316,26 @@
     for a, (stage, out) in enumerate(grads_io):
         arrived(stage.at[:, pl.ds(0, groups - 1)], out_send.at[a])
         arrived(out, out_recv.at[a])
-    arrived(dq_stage.at[:, pl.ds(0, count - 1)], out_send.at[2])
-    arrived(dq_out, out_recv.at[2])
+    arrived(dq_send.at[:, pl.ds(0, groups - 1)], dq_out_send.at[1])
+    arrived(dq_out.at[1], dq_out_recv.at[1])
+    for side, ok, there in sides:
+        @pl.when(ok)
+        def _():
+            slot = (2, 0)[side]
+            arrived(dq_send.at[:, pl.ds(0, groups)], dq_out_send.at[slot])
+            arrived(dq_out.at[(0, 2)[side]], dq_out_recv.at[(0, 2)[side]])
+
+    def finish_sums(i, carry):
+        h, rest = i // (kv_n * z_n), lax.rem(i, kv_n * z_n)
+        owner, plane = rest // z_n, lax.rem(rest, z_n)
+
+        @pl.when((plane < z - 1) | (plane > z + 1))
+        def _():
+            arrived(dq_send.at[h, pl.ds((owner * z_n + plane) * c_n, c_n)], sum_send.at[h, owner, plane])
+
+        return carry
+
+    lax.fori_loop(0, heads * kv_n * z_n, finish_sums, 0)
 
 
 def fused(q, g, k, v, aux, key_total, kv_n, z_n, c_n):
@@ -268,19 +352,20 @@
         in_specs=[any_space] * 5,
         out_specs=[any_space] * 3,
         out_shape=[
-            jax.ShapeDtypeStruct((z_n, owned, total), low),
+            jax.ShapeDtypeStruct((3, owned, total), low),
             jax.ShapeDtypeStruct((keys, total), low),
             jax.ShapeDtypeStruct((keys, total), low),
         ],
         scratch_shapes=[pltpu.VMEM((heads, z_n, c_n * part, DH), low)] * 2
         + [pltpu.VMEM((z_n, c_n) + aux.shape[1:], jnp.float32)]
         + [pltpu.VMEM((heads, groups, keys, DH), low)] * 2
-        + [pltpu.VMEM((heads, z_n * groups, owned, DH), low)]
+        + [pltpu.VMEM((heads, z_n * groups, owned, DH), kind) for kind in (jnp.float32, low, low)]
         + [pltpu.VMEM((heads, groups, keys, DH), low)] * 2
         + [pltpu.VMEM((groups, keys, DH), jnp.float32)] * 2
         + [
             dma((heads, 2)), dma((2,)), dma((heads, z_n, 2)), dma((2, 2)), dma((2,)), dma((heads, z_n, 2)),
-            dma((z_n,)), dma((2,)), dma, dma((z_n,)), dma((3,)), dma((3,)),
+            dma((z_n,)), dma((2,)), dma, dma((z_n,)), dma((2,)), dma((2,)),
+            dma((heads, kv_n, z_n)), dma((heads, kv_n, z_n)), dma((3,)), dma((3,)),
         ],
         compiler_params=pltpu.CompilerParams(
             collective_id=0, has_side_effects=True, vmem_limit_bytes=48 * 2**20
@@ -313,7 +398,10 @@
     aux = jnp.stack([own(stats, near).T, delta.T], axis=1)
     aux = aux.reshape(c_n, 2 * near // c_n, stats.shape[0])
     dq, dk, dv = fused(queries, out_grad, keys, values, aux, key_total, kv_n, z_n, c_n)
-    return jnp.sum(dq.astype(jnp.float32), axis=0), dk.astype(jnp.float32), dv.astype(jnp.float32)
+    z = lax.axis_index("z")
+    dq = dq.astype(jnp.float32)
+    dq = dq[1] + jnp.where(z > 0, dq[0], 0.0) + jnp.where(z < z_n - 1, dq[2], 0.0)
+    return dq, dk.astype(jnp.float32), dv.astype(jnp.float32)
 
 
 def solution(mesh):

time: 248 us -> 222 us (0.90)
  Pallas kernels: 231 us -> 201 us
  other arithmetic: 12.1 us -> 17.7 us
    pallas_call x1, Pallas kernels: 231 us -> 201 us  [fused(): pl.pallas_call(functools.partial(fused_kernel, key_total), in_specs=[any_...]
    convert_element_type x2 -> x3, other arithmetic: 5.02 us -> 10.3 us  [the longest x1 5.31 us: on_device(): dq = dq.astype(jnp.float32)]
    add x0 -> x1, other arithmetic: none -> 4.78 us  [on_device(): dq[1] + jnp.where(z > 0, dq[0], 0.0) + jnp.where(z < z_n - 1, dq[2], 0.0)]
    reduce_sum x1 -> x0, other arithmetic: 4.47 us -> none  [on_device(): jnp.sum(dq.astype(jnp.float32), axis=0)]
where the time goes in v2:
time: 222 us
  Pallas kernels  201 us (91%)
  other arithmetic  17.7 us (8%)
    pallas_call x1, Pallas kernels, fused(): pl.pallas_call(functools.partial(fused_kernel, key_total), in_specs=[any_...  201 us
    convert_element_type x1, other arithmetic, on_device(): dq = dq.astype(jnp.float32)  5.31 us
    convert_element_type x2, other arithmetic, on_device(): return (dq, dk.astype(jnp.float32), dv.astype(jnp.float32))  5 us
    add x1, other arithmetic, on_device(): dq[1] + jnp.where(z > 0, dq[0], 0.0) + jnp.where(z < z_n - 1, dq[2], 0.0)  4.78 us

profile of v2, /device:TPU:0, one launch (start us, length us, event | category | flops | bytes accessed | tf_op | source)
XLA Modules:
  0.0 221.7 jit_solution(2682448672395147404)
XLA Ops:
  0.6 0.0 copy-start
  0.7 2.0 multiply_bitcast_fusion
  2.6 0.5 copy.17
  3.1 0.6 reduce_sum.9
  3.7 0.0 copy-done
  3.7 0.1 copy.16
  3.9 0.2 copy.15
  4.1 201.2 %shard_map.85 = (bf16[3,128,4096]{2,1,0:T(8,128)(2,1)}, bf16[256,4096]{1,0:T(8,128)(2,1)S(1)}, bf16[256,4096]{1,0:T(8,128)(2,1)S(1)}) custom-call(bf16[512,4096]{1,0:T(8,128)(2,1)} %q_in.1, bf16[512,4096]{1,0:T(8,128)(2,1)} %g_in.1, bf16[256,4096]{1,0:T(8,128)(2,1)} %k_in.1, bf16[256,4096]{1,0:T(8,128)(2,1)} %v_in.1, f32[2,8,512]{2,1,0:T(8,128)S(1)} %reshape.20.aux_in), custom_call_target="tpu_custom_call" | custom-call | flops 43000000512 | bytes 30000000 | tf_op jit(solution)/shard_map/pallas_call | solution.py:350
  205.3 0.0 copy-start.1
  205.3 1.3 copy-done.1
  206.6 5.3 %convert_element_type.17 = f32[3,128,4096]{2,1,0:T(8,128)} convert(bf16[3,128,4096]{2,1,0:T(8,128)(2,1)} %get-tuple-element.6) | non-fusion elementwise | flops 1572864 | bytes 9437184 | tf_op jit(solution)/shard_map/convert_element_type | solution.py:402
  212.0 0.0 copy-start.2
  212.0 4.8 %fusion.1 = f32[128,4096]{1,0:T(8,128)} fusion(f32[3,128,4096]{2,1,0:T(8,128)} %convert_element_type.17, pred[]{:T(512)S(6)} %lt.12, pred[]{:T(512)S(6)} %gt.3), kind=kLoop, calls=%fused_computation.2 | loop fusion | flops 2097152 | bytes 8388610 | tf_op jit(solution)/shard_map/add | solution.py:403
  216.7 0.0 copy-done.2
  216.7 2.5 %convert_element_type.18 = f32[256,4096]{1,0:T(8,128)} convert(bf16[256,4096]{1,0:T(8,128)(2,1)S(1)} %copy-done.2) | non-fusion elementwise | flops 1048576 | bytes 6291456 | tf_op jit(solution)/shard_map/convert_element_type | solution.py:404
  219.2 2.5 %convert_element_type.19 = f32[256,4096]{1,0:T(8,128)} convert(bf16[256,4096]{1,0:T(8,128)(2,1)S(1)} %get-tuple-element.8) | non-fusion elementwise | flops 1048576 | bytes 6291456 | tf_op jit(solution)/shard_map/convert_element_type | solution.py:404
  (3 shorter events, 0.1 us)
Async XLA Ops:
  0.6 3.1 %copy-start = (f32[512,32]{0,1:T(8,128)S(1)}, f32[512,32]{0,1:T(8,128)}, u32[]{:S(2)}) copy-start(f32[512,32]{0,1:T(8,128)} %param.11) | copy-start | bytes 196612
  205.3 1.3 copy-start.1
  212.0 4.8 %copy-start.2 = (bf16[256,4096]{1,0:T(8,128)(2,1)S(1)}, bf16[256,4096]{1,0:T(8,128)(2,1)}, u32[]{:S(2)}) copy-start(bf16[256,4096]{1,0:T(8,128)(2,1)} %copy-done.1) | copy-start | bytes 6291460
